TPU v7x, 32 devices: a whole 2x2x4 slice. The times are simulated.
32 devices in a mesh: groups: 2 (over y), dp: 16 (over z, x, core).
Axes of the slice: x: 2, y: 2, z: 4, core: 2. Of those that a mesh axis runs over, the one named last changes fastest.
Arguments:
- query_states: bfloat16 [128, 128, 2048], P(('groups', 'dp')), parts along dimension 0, may hold values from -4.5 to 4.5
- key_states: bfloat16 [128, 128, 512], P(('groups', 'dp')), parts along dimension 0, may hold values from -4.5 to 4.5
- value_states: bfloat16 [128, 128, 512], P(('groups', 'dp')), parts along dimension 0, may hold values from -56 to 56
- out_weight: bfloat16 [2048, 2048], P('dp'), may hold values from -0.125 to 0.125
- token_ids: int32 [128, 128], P(('groups', 'dp')), parts along dimension 0, may hold values from 0 to 31999, as said below
- keep_flags: int32 [128], P(('groups', 'dp')), parts along dimension 0, may hold values from 0 to 1, as said below
- list_ids: int32 [128, 128], P(('groups', 'dp')), parts along dimension 0, may hold values from 0 to 1023, as said below
- owner_map: int32 [2048], P('groups'), parts along dimension 0, may hold values from 0 to 15, as said below
Outputs:
- doc_vectors: bfloat16 [96, 2048], P(('groups', 'dp')), parts along dimension 0
- token_vectors: bfloat16 [16384, 2048], P(('groups', 'dp')), parts along dimension 0
- token_keys: int32 [16384], P(('groups', 'dp')), parts along dimension 0
There are 2 independent parts, one for each index of `groups`. A program takes and returns all parts, laid end to end along the dimension named above; an argument that names none is the same for every part. Nothing has to cross between parts.
Inputs may be any that keep to these rules, and one draw needn't show every extreme that they name: `token_ids`: in each document the ids are 0 exactly from its length on, and its length lies between 96 and 128. `keep_flags`: exactly 48 documents have the flag 1. `list_ids`: the tokens of the 4 documents of one index of dp name lists of any one owner between 16 and 48 times, exactly 48 times for some owner; over all 64 documents the lists of each owner are named exactly 512 times. `owner_map`: every owner holds exactly 64 lists.
All inputs are finite; a program needn't handle non-finite values.
Results may differ from a plain program's by a relative error of at most 0.0057.
Values may be sent and summed in bfloat16 or wider, within the bound.
A program may use at most 64 MiB of HBM per device.

v0:
```python
import math

import jax
import jax.numpy as jnp
from jax import lax
from jax.sharding import PartitionSpec as P

HEAD_DIM = 128


def carried_in(part, axis, combine, identity):
    place = lax.axis_index(axis)
    gathered = lax.all_gather(part, axis)
    state = jnp.zeros_like(part) + jnp.asarray(identity, part.dtype)

    def one(lap, state):
        return combine(state, lax.dynamic_index_in_dim(gathered, lap, 0, False))

    return lax.fori_loop(0, place, one, state)


def add_counts(earlier, later):
    return earlier + later


def normalize(values):
    return (values * lax.rsqrt(jnp.mean(values * values, axis=-1, keepdims=True) + 1e-06)).astype(
        jnp.bfloat16
    )


def attend(query_states, key_states, value_states, token_ids):
    doc_count, length, features = query_states.shape
    kv_features = key_states.shape[2]
    kv_count = kv_features // HEAD_DIM
    group_size = features // kv_features
    queries = query_states.reshape(doc_count, length, kv_count, group_size, HEAD_DIM)
    keys_split = key_states.reshape(doc_count, length, kv_count, HEAD_DIM)
    values_split = value_states.reshape(doc_count, length, kv_count, HEAD_DIM)
    scores = jnp.einsum(
        "nqhgd,nshd->nhgqs", queries, keys_split, preferred_element_type=jnp.float32
    ) / math.sqrt(HEAD_DIM)
    present = token_ids != 0
    scores = jnp.where(present[:, None, None, None, :], scores, -jnp.inf)
    row_max = jnp.max(scores, axis=-1, keepdims=True)
    weights = jnp.exp(scores - row_max)
    weights = (weights / jnp.sum(weights, axis=-1, keepdims=True)).astype(jnp.bfloat16)
    attended = jnp.einsum(
        "nhgqs,nshd->nqhgd", weights, values_split, preferred_element_type=jnp.float32
    )
    attended = attended.reshape(doc_count, length, features).astype(jnp.bfloat16)
    counts = jnp.sum(present.astype(jnp.float32), axis=1)
    pooled_attended = (
        jnp.einsum(
            "nt,ntf->nf", present.astype(jnp.bfloat16), attended, preferred_element_type=jnp.float32
        )
        / counts[:, None]
    )
    return (attended, pooled_attended)


def project(rows, pooled_attended, out_weight):
    piece = lax.all_gather(out_weight, "dp", axis=0, tiled=True)
    row_sum = jnp.dot(rows, piece, preferred_element_type=jnp.float32)
    pooled_sum = jnp.dot(
        pooled_attended, piece.astype(jnp.float32), precision=lax.Precision.HIGHEST
    )
    return (row_sum, pooled_sum)


def send_to_owners(rows, usable, sort_keys, owners, axis_size):
    row_count, width = rows.shape
    capacity = 3 * row_count // (2 * axis_size)
    owner_index = jnp.arange(axis_size, dtype=jnp.int32)
    member = ((owners[:, None] == owner_index[None, :]) & usable[:, None]).astype(jnp.int32)
    running = jnp.cumsum(member, axis=0)
    within = jnp.take_along_axis(running, owners[:, None], axis=1)[:, 0] - 1
    slots = jnp.where(usable, owners * capacity + within, axis_size * capacity)
    packed = jnp.zeros((axis_size * capacity, width), rows.dtype).at[slots].set(rows, mode="drop")
    packed_keys = (
        jnp.full((axis_size * capacity,), -1, jnp.int32).at[slots].set(sort_keys, mode="drop")
    )
    arrived, arrived_keys = (
        lax.all_to_all(
            packed.reshape(axis_size, capacity, width),
            "dp",
            split_axis=0,
            concat_axis=0,
            tiled=True,
        ),
        lax.all_to_all(
            packed_keys.reshape(axis_size, capacity), "dp", split_axis=0, concat_axis=0, tiled=True
        ),
    )
    arrived = arrived.reshape(-1, width)
    arrived_keys = arrived_keys.reshape(-1)
    filled = arrived_keys >= 0
    smaller = jnp.sum(filled[None, :] & (arrived_keys[None, :] < arrived_keys[:, None]), axis=1)
    targets = jnp.where(filled, smaller, row_count)
    sorted_rows = jnp.zeros((row_count, width), rows.dtype).at[targets].set(arrived, mode="drop")
    sorted_keys = jnp.full((row_count,), -1, jnp.int32).at[targets].set(arrived_keys, mode="drop")
    return (sorted_rows, sorted_keys)


def shards(
    query_states, key_states, value_states, out_weight, token_ids, keep_flags, list_ids, owner_map
):
    axis_size = lax.axis_size("dp")
    my_index = lax.axis_index("dp")
    slot_count = keep_flags.shape[0]
    kept_slots = 3 * slot_count // 4
    before = carried_in(keep_flags, "dp", add_counts, jnp.zeros_like(keep_flags))
    totals = lax.psum(keep_flags.astype(jnp.float32), "dp").astype(jnp.int32)
    earlier = jnp.cumsum(totals) - totals
    occupied = keep_flags == 1
    position = (earlier + before).astype(jnp.int32)
    doc_rank = jnp.where(occupied, position, -1)
    attended, pooled_attended = attend(query_states, key_states, value_states, token_ids)
    doc_count, length, features = attended.shape
    flat_rows = attended.reshape(doc_count * length, features)
    owners = jnp.take(owner_map, list_ids, axis=0).reshape(-1)
    usable_grid = occupied[:, None] & (token_ids != 0)
    positions = jnp.arange(length, dtype=jnp.int32)
    sort_keys = jnp.where(usable_grid, doc_rank[:, None] * length + positions[None, :], -1).reshape(
        -1
    )
    usable = usable_grid.reshape(-1)
    projected, pooled = project(flat_rows, pooled_attended, out_weight)
    unit_tokens = normalize(projected)
    token_vectors, token_keys = send_to_owners(unit_tokens, usable, sort_keys, owners, axis_size)
    unit_docs = normalize(pooled)
    every_doc, every_rank = (
        lax.all_gather(unit_docs, "dp", axis=0, tiled=True),
        lax.all_gather(doc_rank, "dp", axis=0, tiled=True),
    )
    wanted = jnp.arange(kept_slots, dtype=jnp.int32) * axis_size + my_index
    picker = (every_rank[None, :] == wanted[:, None]).astype(jnp.bfloat16)
    doc_vectors = jnp.dot(picker, every_doc, preferred_element_type=jnp.float32).astype(
        jnp.bfloat16
    )
    return (doc_vectors, token_vectors, token_keys)


def solution(mesh):
    return jax.shard_map(
        shards,
        mesh=mesh,
        in_specs=(
            P(("groups", "dp"), None, None),
            P(("groups", "dp"), None, None),
            P(("groups", "dp"), None, None),
            P("dp", None),
            P(("groups", "dp"), None),
            P(("groups", "dp")),
            P(("groups", "dp"), None),
            P("groups"),
        ),
        out_specs=(P(("groups", "dp"), None), P(("groups", "dp"), None), P(("groups", "dp"))),
        check_vma=False,
    )
```

profile of v0, /device:TPU:0, one launch (start us, length us, event | category | flops | bytes accessed | tf_op | source)
XLA Modules:
  0.0 237.1 jit_solution(729401904148163551)
XLA Ops:
  8.6 35.5 %psum.7 = f32[4]{0:T(128)S(1)} all-reduce(f32[4]{0:T(128)S(1)} %convert_element_type.46), channel_id=1, replica_groups=mesh['groups'=2,'dp'=16] {'dp'}, use_global_device_ids=true, to_apply=%region_0.1 | all-reduce | flops 4 | bytes 32 | tf_op jit(solution)/shard_map/psum | solution.py:113
  44.1 1.2 dynamic-slice
  46.0 0.9 dynamic-update-slice
  46.9 8.3 %all-reduce = s32[64]{0:T(128)S(1)} all-reduce(s32[64]{0:T(128)S(1)} %dynamic-update-slice), channel_id=2, replica_groups=mesh['groups'=2,'dp'=16] {'dp'}, use_global_device_ids=true, to_apply=%add | all-reduce | flops 64 | bytes 512
  56.1 2.3 gather_fusion
  59.8 0.8 select_bitcast_fusion
  61.2 1.2 reduce-window.20
  62.8 4.5 %gather_fusion.1 = s32[512]{0:T(512)S(1)} fusion(s32[512,16]{0,1:T(8,128)S(1)} %bitcast_bitcast_fusion, s32[512]{0:T(512)S(1)} %bitcast.79), kind=kCustom, calls=%fused_computation.1 | custom fusion | bytes 8192 | tf_op jit(solution)/shard_map/jit(take_along_axis)/gather | solution.py:77
  67.3 2.4 %scatter_custom_fusion = s32[768]{0:T(1024)S(1)} fusion(s32[512]{0:T(512)S(1)} %bitcast.89, s32[512]{0:T(512)S(1)} %get-tuple-element.35, s32[]{:T(128)} %constant.29.clone.1), kind=kCustom, calls=%fused_computation.67 | custom fusion | bytes 3076 | tf_op jit(solution)/shard_map/scatter | solution.py:81
  70.5 6.3 %all-to-all-start = ((s32[16,1,48]{2,1,0:T(1,128)}), s32[16,1,48]{2,1,0:T(1,128)S(1)}, u32[]{:S(2)}, u32[]{:S(2)}) async-start(s32[16,1,48]{2,1,0:T(1,128)} %all_to_all.9), calls=%async_computation | async-start | bytes 16384 | tf_op jit(solution)/shard_map/all_to_all | solution.py:91
  76.8 1.0 copy.40
  77.8 3.3 %reshape.386 = bf16[4,128,4,4,128]{4,3,2,1,0:T(4,128)(2,1)S(1)} reshape(bf16[4,128,2048]{2,1,0:T(8,128)(2,1)} %param.10) | data formatting | bytes 4194304 | tf_op jit(solution)/shard_map/reshape | solution.py:37
  82.0 1.7 fusion.45
  84.4 2.9 %copy.32 = bf16[4,128,4,4,128]{4,3,2,1,0:T(4,128)(2,1)} copy(bf16[4,128,4,4,128]{1,4,3,2,0:T(8,128)(2,1)S(1)} %bitcast.80) | data formatting | bytes 4194304 | tf_op jit(solution)/shard_map/convert_element_type | solution.py:51
  87.3 4.5 %convert_element_type.57 = bf16[512,2048]{1,0:T(8,128)(2,1)} reshape(bf16[4,128,4,4,128]{4,3,2,1,0:T(4,128)(2,1)} %copy.32) | data formatting | bytes 4194304 | tf_op jit(solution)/shard_map/convert_element_type | solution.py:51
  91.8 10.5 %multiply_reduce_fusion = (f32[512]{0:T(512)S(1)}, f32[512,2048]{1,0:T(8,128)}) fusion(bf16[512,2048]{1,0:T(8,128)(2,1)} %convert_element_type.57, bf16[2048,2048]{1,0:T(8,128)(2,1)} %all-gather.4.cloned.1.call-done), kind=kOutput, calls=%fused_computation.13 | convolution fusion | flops 4297063936 | bytes 14682112 | tf_op jit(solution)/shard_map/dot_general | solution.py:64
  102.3 7.4 %scatter_custom_fusion.1 = bf16[768,2048]{1,0:T(8,128)(2,1)} fusion(s32[512]{0:T(512)S(1)} %bitcast.90, f32[512,2048]{1,0:T(8,128)} %get-tuple-element.45, f32[512]{0:T(512)S(1)} %add_rsqrt_fusion, bf16[]{:T(256)} %constant.40.clone.1), kind=kCustom, calls=%fused_computation.18 | custom fusion | flops 2097152 | bytes 7342082 | tf_op jit(solution)/shard_map/scatter | solution.py:79
  109.7 6.0 %all-to-all-start.1 = ((bf16[16,48,2048]{2,1,0:T(8,128)(2,1)}), bf16[16,48,2048]{2,1,0:T(8,128)(2,1)}, u32[]{:S(2)}, u32[]{:S(2)}) async-start(bf16[16,48,2048]{2,1,0:T(8,128)(2,1)} %bitcast.24), calls=%async_computation.1 | async-start | bytes 6291456 | tf_op jit(solution)/shard_map/all_to_all | solution.py:84
  115.9 71.5 %all-reduce.1 = s32[64]{0:T(128)S(1)} all-reduce(s32[64]{0:T(128)S(1)} %dynamic-update-slice.1), channel_id=1, replica_groups=mesh['groups'=2,'dp'=16] {'dp'}, use_global_device_ids=true, to_apply=%add.1 | all-reduce | flops 64 | bytes 512
  190.1 3.9 %scatter_custom_fusion.3 = s32[512]{0:T(512)} fusion(s32[768]{0:T(1024)S(1)} %fusion.28, s32[768]{0:T(1024)S(1)} %reshape.438, s32[]{:T(128)} %constant.29.clone.1), kind=kCustom, calls=%fused_computation.72 | custom fusion | bytes 2052 | tf_op jit(solution)/shard_map/scatter | solution.py:101
  194.0 5.9 %multiply_reduce_fusion.1 = (f32[4]{0:T(128)S(1)}, f32[4,2048]{1,0:T(4,128)S(1)}) fusion(bf16[2048,2048]{1,0:T(8,128)(2,1)} %all-gather.4.cloned.1.call-done, f32[4,1,2048]{2,1,0:T(1,128)S(1)} %fusion.26, f32[4]{0:T(128)S(1)} %convert_reduce_fusion.1), kind=kOutput, calls=%fused_computation.40 | convolution fusion | flops 201351168 | bytes 8454176 | tf_op jit(solution)/shard_map/dot_general | solution.py:65
  200.0 20.1 %all-gather.1 = bf16[16,4,2048]{2,1,0:T(4,128)(2,1)S(1)} all-gather(bf16[1,4,2048]{2,1,0:T(4,128)(2,1)S(1)} %fusion.24), channel_id=1, replica_groups=mesh['groups'=2,'dp'=16] {'dp'}, dimensions={0}, use_global_device_ids=true | all-gather | bytes 278528 | tf_op jit(solution)/shard_map/all_gather | solution.py:133
  220.1 0.8 convolution_convert_fusion
  220.9 9.3 %scatter_custom_fusion.2 = bf16[512,2048]{1,0:T(8,128)(2,1)} fusion(s32[768]{0:T(1024)S(1)} %fusion.28, bf16[768,2048]{1,0:T(8,128)(2,1)} %bitcast.25, bf16[]{:T(256)} %constant.40.clone.1), kind=kCustom, calls=%fused_computation.28 | custom fusion | bytes 2097664 | tf_op jit(solution)/shard_map/scatter | solution.py:100
  (56 shorter events, 10.1 us)
Async XLA Ops:
  7.2 49.0 %copy-start = (s32[1024]{0:T(1024)S(1)}, s32[1024]{0:T(1024)}, u32[]{:S(2)}) copy-start(s32[1024]{0:T(1024)} %param.17) | copy-start | bytes 12292
  7.2 69.6 %copy-start.1 = (bf16[4,128,512]{2,1,0:T(8,128)(2,1)S(1)}, bf16[4,128,512]{2,1,0:T(8,128)(2,1)}, u32[]{:S(2)}) copy-start(bf16[4,128,512]{2,1,0:T(8,128)(2,1)} %param.12) | copy-start | bytes 1572868
  7.2 84.6 %all-gather.4.cloned.1.call-start = ((), (), s32[]{:S(2)}) async-start(), calls=%async_computation.2 | async-start | bytes 8912896 | tf_op jit(solution)/shard_map/all_gather | solution.py:63
  67.3 13.8 %copy-start.2 = (bf16[4,128,512]{2,1,0:T(8,128)(2,1)S(1)}, bf16[4,128,512]{2,1,0:T(8,128)(2,1)}, u32[]{:S(2)}) copy-start(bf16[4,128,512]{2,1,0:T(8,128)(2,1)} %param.11) | copy-start | bytes 1572868
  70.5 39.2 %all-to-all-start = ((s32[16,1,48]{2,1,0:T(1,128)}), s32[16,1,48]{2,1,0:T(1,128)S(1)}, u32[]{:S(2)}, u32[]{:S(2)}) async-start(s32[16,1,48]{2,1,0:T(1,128)} %all_to_all.9), calls=%async_computation | async-start | bytes 16384 | tf_op jit(solution)/shard_map/all_to_all | solution.py:91
  82.0 1.7 copy-start.3
  109.7 111.2 %all-to-all-start.1 = ((bf16[16,48,2048]{2,1,0:T(8,128)(2,1)}), bf16[16,48,2048]{2,1,0:T(8,128)(2,1)}, u32[]{:S(2)}, u32[]{:S(2)}) async-start(bf16[16,48,2048]{2,1,0:T(8,128)(2,1)} %bitcast.24), calls=%async_computation.1 | async-start | bytes 6291456 | tf_op jit(solution)/shard_map/all_to_all | solution.py:84
Sparse Core Ops, SparseCore 0:
  10.2 78.0 all-gather.3
where the time goes:
time: 238 us; the launch traced here: 237 us
  blocking collectives  135 us (57%)
  local copies, waits for them, and re-layouts  38.4 us (16%)
  matrix products  19.2 us (8%)
  other arithmetic  16.1 us (7%)
  between operations  14.9 us (6%)
  starting transfers between devices  12.3 us (5%)
    unnamed x2, blocking collectives  79.8 us
    psum x1, blocking collectives, shards(): totals = lax.psum(keep_flags.astype(jnp.float32), 'dp').astype(jnp.int32)  35.5 us
    all_gather x1, blocking collectives, shards(): lax.all_gather(unit_docs, 'dp', axis=0, tiled=True)  20.1 us
    dot_general x1, matrix products, project(): row_sum = jnp.dot(rows, piece, preferred_element_type=jnp.float32)  10.5 us
    scatter x1, local copies, waits for them, and re-layouts, send_to_owners(): jnp.zeros((row_count, width), rows.dtype).at[targets]  9.31 us
    convert_element_type x2, local copies, waits for them, and re-layouts, attend(): attended.reshape(doc_count, length, features).astype(jnp.bfloat16)  7.39 us
    scatter x1, other arithmetic, send_to_owners(): jnp.zeros((axis_size * capacity, width), rows.dtype).at[slots]  7.38 us
    all_to_all x1, starting transfers between devices, send_to_owners(): lax.all_to_all(packed_keys.reshape(axis_size, capacity), 'dp', split_axis...  6.32 us
  transfers between devices with their start and end apart: 3, of which 0 were waited for; matrix products, arithmetic and copies ran while one was open for 27% of the time, Pallas kernels for 0%

commit v1 on v0

v1 whole, which is shorter than its diff:
```python
import math

import jax
import jax.numpy as jnp
from jax import lax
from jax.sharding import PartitionSpec as P

HEAD_DIM = 128
F32 = jnp.float32
BF16 = jnp.bfloat16


def normalize(values):
    return (values * lax.rsqrt(jnp.mean(values * values, axis=-1, keepdims=True) + 1e-06)).astype(BF16)


def attend(query_states, key_states, value_states, token_ids):
    doc_count, length, features = query_states.shape
    kv_features = key_states.shape[2]
    kv_count = kv_features // HEAD_DIM
    group_size = features // kv_features
    queries = query_states.reshape(doc_count, length, kv_count, group_size, HEAD_DIM)
    keys_split = key_states.reshape(doc_count, length, kv_count, HEAD_DIM)
    values_split = value_states.reshape(doc_count, length, kv_count, HEAD_DIM)
    scores = jnp.einsum(
        "nqhgd,nshd->nhgqs", queries, keys_split, preferred_element_type=F32
    ) / math.sqrt(HEAD_DIM)
    present = token_ids != 0
    scores = jnp.where(present[:, None, None, None, :], scores, -jnp.inf)
    row_max = jnp.max(scores, axis=-1, keepdims=True)
    weights = jnp.exp(scores - row_max)
    weights = (weights / jnp.sum(weights, axis=-1, keepdims=True)).astype(BF16)
    attended = jnp.einsum("nhgqs,nshd->nqhgd", weights, values_split, preferred_element_type=F32)
    attended = attended.reshape(doc_count, length, features).astype(BF16)
    counts = jnp.sum(present.astype(F32), axis=1)
    pooled = (
        jnp.einsum("nt,ntf->nf", present.astype(BF16), attended, preferred_element_type=F32)
        / counts[:, None]
    )
    return attended, pooled


def exclusive_rows(mask):
    size = mask.shape[-1]
    at = jnp.arange(size, dtype=jnp.int32)
    upper = (at[:, None] < at[None, :]).astype(BF16)
    return jnp.dot(mask.astype(BF16), upper, preferred_element_type=F32).astype(jnp.int32)


def routing(codes, flags, me):
    n, docs, length = codes.shape
    place = jnp.arange(docs, dtype=jnp.int32)[None, :] * n + jnp.arange(n, dtype=jnp.int32)[:, None]
    place = place.reshape(-1)
    kept = flags.reshape(-1) == 1
    before = (place[None, :] < place[:, None]) & kept[None, :]
    rank = jnp.where(kept, jnp.sum(before.astype(jnp.int32), axis=1), -1)
    mine = (codes == me).reshape(n * docs, length)
    inner = exclusive_rows(mine)
    count = jnp.sum(mine.astype(jnp.int32), axis=1)
    earlier_rank = jnp.sum(jnp.where(before, count[None, :], 0), axis=1)
    position = earlier_rank[:, None] + inner
    by_source = count.reshape(n, docs)
    doc = jnp.arange(docs, dtype=jnp.int32)
    earlier_doc = jnp.sum(
        jnp.where(doc[None, None, :] < doc[None, :, None], by_source[:, None, :], 0), axis=2
    )
    slot = earlier_doc.reshape(-1)[:, None] + inner
    keys = rank[:, None] * length + jnp.arange(length, dtype=jnp.int32)[None, :]
    return rank, mine, position, slot, keys


def shards(
    query_states, key_states, value_states, out_weight, token_ids, keep_flags, list_ids, owner_map
):
    n = lax.axis_size("dp")
    me = lax.axis_index("dp").astype(jnp.int32)
    docs, length, features = query_states.shape
    rows = docs * length
    cap = 3 * rows // (2 * n)
    weight = lax.all_gather(out_weight, "dp", axis=0, tiled=True)

    lists = owner_map.shape[0]
    hit = list_ids.reshape(-1)[:, None] == jnp.arange(lists, dtype=jnp.int32)[None, :]
    owners = jnp.sum(jnp.where(hit, owner_map[None, :], 0), axis=1).reshape(docs, length)
    codes = jnp.where((keep_flags == 1)[:, None] & (token_ids != 0), owners, -1)
    info = jnp.concatenate([codes, jnp.broadcast_to(keep_flags[:, None], (docs, length))], axis=0)
    every = lax.all_gather(info, "dp")
    rank, mine, position, slot, keys = routing(every[:, :docs], every[:, docs:, 0], me)

    flat = codes.reshape(-1)
    member = (flat[None, :] == jnp.arange(n, dtype=jnp.int32)[:, None])
    at = jnp.arange(rows, dtype=jnp.int32)
    tri = (at[:, None] < at[None, :]).astype(BF16)
    within = jnp.dot(member.astype(BF16), tri, preferred_element_type=F32).astype(jnp.int32)
    pick = (
        member[:, None, :]
        & (within[:, None, :] == jnp.arange(cap, dtype=jnp.int32)[None, :, None])
    ).astype(BF16).reshape(n * cap, rows)

    attended, pooled = attend(query_states, key_states, value_states, token_ids)
    packed = jnp.dot(pick, attended.reshape(rows, features), preferred_element_type=F32).astype(BF16)
    arrived = lax.all_to_all(
        packed.reshape(n, cap, features), "dp", split_axis=0, concat_axis=0, tiled=True
    ).reshape(n * cap, features)
    high = pooled.astype(BF16)
    low = (pooled - high.astype(F32)).astype(BF16)
    every_doc = lax.all_gather(jnp.concatenate([high, low], axis=0), "dp")
    every_doc = jnp.concatenate([every_doc[:, :docs], every_doc[:, docs:]], axis=2).reshape(
        n * docs, 2 * features
    )

    mine_s = mine.reshape(n, rows)
    slot_s = jnp.where(mine_s, slot.reshape(n, rows), -1)
    fits = slot_s[:, None, :] == jnp.arange(cap, dtype=jnp.int32)[None, :, None]
    slot_position = jnp.sum(
        jnp.where(fits, position.reshape(n, 1, rows) + 1, 0), axis=2
    ).reshape(-1) - 1
    slot_key = jnp.sum(jnp.where(fits, keys.reshape(n, 1, rows) + 1, 0), axis=2).reshape(-1)
    order = jnp.arange(rows, dtype=jnp.int32)[:, None] == slot_position[None, :]
    token_keys = jnp.sum(jnp.where(order, slot_key[None, :], 0), axis=1) - 1
    sorted_rows = jnp.dot(order.astype(BF16), arrived, preferred_element_type=F32).astype(BF16)
    token_vectors = normalize(jnp.dot(sorted_rows, weight, preferred_element_type=F32))

    kept_slots = 3 * docs // 4
    wanted = jnp.arange(kept_slots, dtype=jnp.int32) * n + me
    picker = (rank[None, :] == wanted[:, None]).astype(BF16)
    chosen = jnp.dot(picker, every_doc, preferred_element_type=F32).astype(BF16)
    parts = jnp.concatenate([chosen[:, :features], chosen[:, features:]], axis=0)
    doc_sum = jnp.dot(parts, weight, preferred_element_type=F32)
    doc_vectors = normalize(doc_sum[:kept_slots] + doc_sum[kept_slots:])
    return (doc_vectors, token_vectors, token_keys)


def solution(mesh):
    return jax.shard_map(
        shards,
        mesh=mesh,
        in_specs=(
            P(("groups", "dp"), None, None),
            P(("groups", "dp"), None, None),
            P(("groups", "dp"), None, None),
            P("dp", None),
            P(("groups", "dp"), None),
            P(("groups", "dp")),
            P(("groups", "dp"), None),
            P("groups"),
        ),
        out_specs=(P(("groups", "dp"), None), P(("groups", "dp"), None), P(("groups", "dp"))),
        check_vma=False,
    )
```

time: 238 us -> 208 us (0.87)
  local copies, waits for them, and re-layouts: 38.4 us -> 14.6 us
  other arithmetic: 16.1 us -> 9.94 us
  matrix products: 19.2 us -> 24.7 us
  starting transfers between devices: 12.3 us -> 7.48 us
    all_gather x1 -> x2, blocking collectives: 20.1 us -> 135 us  [the longest x1 101 us: shards(): every = lax.all_gather(info, 'dp')]
    unnamed x2 -> x0, blocking collectives: 79.8 us -> none
    psum x1 -> x0, blocking collectives: 35.5 us -> none  [shards(): totals = lax.psum(keep_flags.astype(jnp.float32), 'dp').astype(jnp.int32)]
    scatter x3 -> x0, local copies, waits for them, and re-layouts: 15.7 us -> none  [the longest x1 9.31 us: send_to_owners(): jnp.zeros((row_count, width), rows.dtype).at[targets]]
    scatter x1 -> x0, other arithmetic: 7.38 us -> none  [send_to_owners(): jnp.zeros((axis_size * capacity, width), rows.dtype).at[slots]]
    gather x2 -> x0, local copies, waits for them, and re-layouts: 6.83 us -> none  [the longest x1 4.54 us: send_to_owners(): within = jnp.take_along_axis(running, owners[:, None], axis=1)[:, 0] - 1]
    dot_general x4 -> x7, matrix products: 17.8 us -> 23.3 us  [the longest x1 12.4 us: shards(): jnp.dot(sorted_rows, weight, preferred_element_type=F32)]
    all_to_all x2 -> x1, starting transfers between devices: 12.3 us -> 7.45 us  [shards(): lax.all_to_all(packed.reshape(n, cap, features), 'dp', split_axis=0, conc...]
  transfers between devices with their start and end apart: 3 -> 2, of which waited for: 0 -> 0; matrix products, arithmetic and copies ran while one was open for 27% -> 16% of each run, Pallas kernels for 0% -> 0%
where the time goes in v1:
time: 208 us; the launch traced here: 207 us
  blocking collectives  135 us (65%)
  matrix products  24.7 us (12%)
  local copies, waits for them, and re-layouts  14.6 us (7%)
  between operations  14.4 us (7%)
  other arithmetic  9.94 us (5%)
  starting transfers between devices  7.48 us (4%)
    all_gather x1, blocking collectives, shards(): every = lax.all_gather(info, 'dp')  101 us
    all_gather x1, blocking collectives, shards(): every_doc = lax.all_gather(jnp.concatenate([high, low], axis=0), 'dp')  34.3 us
    dot_general x1, matrix products, shards(): jnp.dot(sorted_rows, weight, preferred_element_type=F32)  12.4 us
    convert_element_type x2, local copies, waits for them, and re-layouts, attend(): attended = attended.reshape(doc_count, length, features).astype(BF16)  7.45 us
    all_to_all x1, starting transfers between devices, shards(): lax.all_to_all(packed.reshape(n, cap, features), 'dp', split_axis=0, conc...  7.45 us
    dot_general x1, matrix products, shards(): jnp.dot(pick, attended.reshape(rows, features), preferred_element_type=F32)  5.15 us
    dot_general x1, matrix products, shards(): doc_sum = jnp.dot(parts, weight, preferred_element_type=F32)  4.57 us
    convert_element_type x2, other arithmetic, normalize(): (values * lax.rsqrt(jnp.mean(values * values, axis=-1, keepdims=True) + 1...  4.49 us
  transfers between devices with their start and end apart: 2, of which 0 were waited for; matrix products, arithmetic and copies ran while one was open for 16% of the time, Pallas kernels for 0%

profile of v1, /device:TPU:0, one launch (start us, length us, event | category | flops | bytes accessed | tf_op | source)
XLA Modules:
  0.0 207.2 jit_solution(4567559013097484948)
XLA Ops:
  7.2 0.7 all-gather.4.cloned.1.call-update
  8.0 2.1 copy.46
  10.0 3.2 %reshape.261 = bf16[4,128,4,4,128]{4,3,2,1,0:T(4,128)(2,1)S(1)} reshape(bf16[4,128,2048]{2,1,0:T(8,128)(2,1)} %param.8) | data formatting | bytes 4194304 | tf_op jit(solution)/shard_map/reshape | solution.py:22
  13.4 0.4 select_reduce_fusion
  13.9 0.7 fusion.5
  14.7 1.7 fusion.32
  16.4 0.7 fusion.11
  17.1 2.9 %copy.36 = bf16[4,128,4,4,128]{4,3,2,1,0:T(4,128)(2,1)} copy(bf16[4,128,4,4,128]{1,4,3,2,0:T(8,128)(2,1)S(1)} %bitcast.56) | data formatting | bytes 4194304 | tf_op jit(solution)/shard_map/convert_element_type | solution.py:34
  20.0 4.6 %convert_element_type.79 = bf16[512,2048]{1,0:T(8,128)(2,1)} reshape(bf16[4,128,4,4,128]{4,3,2,1,0:T(4,128)(2,1)} %copy.36) | data formatting | bytes 4194304 | tf_op jit(solution)/shard_map/convert_element_type | solution.py:34
  24.7 0.3 fusion.12
  25.0 5.1 %convolution_convert_fusion.1 = bf16[768,2048]{1,0:T(8,128)(2,1)} fusion(pred[768,512]{1,0:T(8,128)(4,1)S(1)} %bitcast.62, bf16[512,2048]{1,0:T(8,128)(2,1)} %convert_element_type.79), kind=kOutput, calls=%fused_computation.10 | convolution fusion | flops 1612185600 | bytes 5636096 | tf_op jit(solution)/shard_map/dot_general | solution.py:101
  30.2 7.4 %all-to-all-start = ((bf16[16,48,2048]{2,1,0:T(8,128)(2,1)}), bf16[16,48,2048]{2,1,0:T(8,128)(2,1)}, u32[]{:S(2)}, u32[]{:S(2)}) async-start(bf16[16,48,2048]{2,1,0:T(8,128)(2,1)} %bitcast.58), calls=%async_computation | async-start | bytes 6291456 | tf_op jit(solution)/shard_map/all_to_all | solution.py:102
  37.8 101.1 %all-gather = s32[128,128]{1,0:T(8,128)S(1)} all-gather(s32[8,128]{1,0:T(8,128)S(1)} %pad_add_fusion), channel_id=2, replica_groups=mesh['groups'=2,'dp'=16] {'dp'}, dimensions={0}, use_global_device_ids=true | all-gather | bytes 69632 | tf_op jit(solution)/shard_map/all_gather | solution.py:87
  138.9 0.3 convert_reduce_fusion
  139.5 0.6 fusion.22
  140.3 34.3 %all-gather.1 = bf16[128,2048]{1,0:T(8,128)(2,1)S(1)} all-gather(bf16[8,2048]{1,0:T(8,128)(2,1)S(1)} %pad_maximum_fusion.1), channel_id=3, replica_groups=mesh['groups'=2,'dp'=16] {'dp'}, dimensions={0}, use_global_device_ids=true | all-gather | bytes 557056 | tf_op jit(solution)/shard_map/all_gather | solution.py:107
  174.6 0.3 fusion.30
  174.8 0.3 pad_maximum_fusion
  176.7 0.7 select_reduce_fusion.2
  177.8 0.6 broadcast_add_fusion.2
  178.7 4.6 %fusion.18 = f32[6,2048]{1,0:T(8,128)S(1)} fusion(bf16[2048,2048]{1,0:T(8,128)(2,1)} %all-gather.4.cloned.1.call-done, bf16[3,2048]{1,0:T(4,128)(2,1)S(1)} %get-tuple-element.18, bf16[3,2048]{1,0:T(4,128)(2,1)S(1)} %get-tuple-element.17), kind=kOutput, calls=%fused_computation.41 | convolution fusion | flops 50380800 | bytes 8462336 | tf_op jit(solution)/shard_map/dot_general | solution.py:129
  183.4 0.7 multiply_convert_fusion.1
  184.1 12.4 %multiply_reduce_fusion = (f32[512]{0:T(512)S(1)}, f32[512,2048]{1,0:T(8,128)}) fusion(bf16[2048,2048]{1,0:T(8,128)(2,1)} %all-gather.4.cloned.1.call-done, bf16[768,2048]{1,0:T(8,128)(2,1)} %bitcast.17, s32[768]{0:T(1024)S(1)} %sub.25), kind=kOutput, calls=%fused_computation.7 | convolution fusion | flops 5909118464 | bytes 15733760 | tf_op jit(solution)/shard_map/dot_general | solution.py:122
  196.6 3.8 %multiply_convert_fusion = bf16[512,2048]{1,0:T(8,128)(2,1)} fusion(f32[512,2048]{1,0:T(8,128)} %get-tuple-element.22, f32[512]{0:T(512)S(1)} %add_rsqrt_fusion), kind=kLoop, calls=%fused_computation.6 | loop fusion | flops 2097152 | bytes 6293504 | tf_op jit(solution)/shard_map/convert_element_type | solution.py:14
  (62 shorter events, 3.3 us)
Async XLA Ops:
  7.2 6.1 %copy-start = (bf16[4,128,512]{2,1,0:T(8,128)(2,1)S(1)}, bf16[4,128,512]{2,1,0:T(8,128)(2,1)}, u32[]{:S(2)}) copy-start(bf16[4,128,512]{2,1,0:T(8,128)(2,1)} %param.9) | copy-start | bytes 1572868
  7.2 171.5 %all-gather.4.cloned.1.call-start = ((), (), s32[]{:S(2)}) async-start(), calls=%async_computation.1 | async-start | bytes 8912896 | tf_op jit(solution)/shard_map/all_gather | solution.py:80
  7.9 5.5 %copy-start.2 = (s32[1024]{0:T(1024)S(1)}, s32[1024]{0:T(1024)}, u32[]{:S(2)}) copy-start(s32[1024]{0:T(1024)} %param.15) | copy-start | bytes 12292
  7.9 5.5 %copy-start.4 = (s32[4,128]{1,0:T(4,128)S(1)}, s32[4,128]{1,0:T(4,128)}, u32[]{:S(2)}) copy-start(s32[4,128]{1,0:T(4,128)} %param.14) | copy-start | bytes 6148
  7.9 5.9 %copy-start.5 = (s32[4]{0:T(128)S(1)}, s32[4]{0:T(128)}, u32[]{:S(2)}) copy-start(s32[4]{0:T(128)} %param.13) | copy-start | bytes 52
  7.9 5.9 %copy-start.3 = (s32[4,128]{1,0:T(4,128)S(1)}, s32[4,128]{1,0:T(4,128)}, u32[]{:S(2)}) copy-start(s32[4,128]{1,0:T(4,128)} %param.12) | copy-start | bytes 6148
  14.7 1.7 copy-start.1
  30.2 154.0 %all-to-all-start = ((bf16[16,48,2048]{2,1,0:T(8,128)(2,1)}), bf16[16,48,2048]{2,1,0:T(8,128)(2,1)}, u32[]{:S(2)}, u32[]{:S(2)}) async-start(bf16[16,48,2048]{2,1,0:T(8,128)(2,1)} %bitcast.58), calls=%async_computation | async-start | bytes 6291456 | tf_op jit(solution)/shard_map/all_to_all | solution.py:102
Sparse Core Ops, SparseCore 0:
  10.2 118.6 all-gather.3

commit v2 on v1

--- a/solution.py
+++ b/solution.py
@@ -1,8 +1,11 @@
+import functools
 import math
 
 import jax
 import jax.numpy as jnp
 from jax import lax
+from jax.experimental import pallas as pl
+from jax.experimental.pallas import tpu as pltpu
 from jax.sharding import PartitionSpec as P
 
 HEAD_DIM = 128
@@ -69,6 +72,181 @@
     return rank, mine, position, slot, keys
 
 
+def exchange_kernel(
+    n, w_ref, rows_ref, docs_ref, info_ref, w_all, rows_all, docs_all, info_all,
+    w_send, w_recv, peer_send, peer_recv, own_sem,
+):
+    me = lax.axis_index("dp")
+    planes = n // 4
+    plane, spot = lax.div(me, 4), lax.rem(me, 4)
+    core, column = lax.rem(spot, 2), lax.div(spot, 2)
+    depth = w_ref.shape[0]
+    mate = me + 1 - 2 * core
+    beside = me + 2 - 4 * column
+
+    barrier = pltpu.get_barrier_semaphore()
+
+    def greet(k, _):
+        pl.semaphore_signal(barrier, inc=1, device_id={"dp": lax.rem(me + k, n)}, device_id_type=pl.DeviceIdType.MESH)
+        return 0
+
+    lax.fori_loop(1, n, greet, 0)
+    pl.semaphore_wait(barrier, n - 1)
+
+    def span(block):
+        return pl.ds(pl.multiple_of(block * depth, depth), depth)
+
+    def block_copy(block, lane, target, source=None):
+        return pltpu.make_async_remote_copy(
+            src_ref=w_all.at[span(block)] if source is None else source,
+            dst_ref=w_all.at[span(block)],
+            send_sem=w_send.at[lane, block],
+            recv_sem=w_recv.at[block],
+            device_id={"dp": target},
+            device_id_type=pl.DeviceIdType.MESH,
+        )
+
+    has_up, has_down = plane < planes - 1, plane > 0
+
+    @pl.when(has_up)
+    def _():
+        block_copy(me, 0, me + 4, w_ref).start()
+
+    @pl.when(has_down)
+    def _():
+        block_copy(me, 1, me - 4, w_ref).start()
+
+    block_copy(me, 2, beside, w_ref).start()
+    block_copy(me, 3, mate, w_ref).start()
+
+    arrays = ((rows_ref, rows_all), (docs_ref, docs_all), (info_ref, info_all))
+    owns = [pltpu.make_async_copy(w_ref, w_all.at[span(me)], own_sem.at[0])]
+    owns.append(pltpu.make_async_copy(rows_ref.at[me], rows_all.at[me], own_sem.at[1]))
+    owns.append(pltpu.make_async_copy(docs_ref, docs_all.at[me], own_sem.at[2]))
+    owns.append(pltpu.make_async_copy(info_ref, info_all.at[me], own_sem.at[3]))
+    for copy in owns:
+        copy.start()
+
+    def peer_copy(which, k, peer, slot):
+        here, there = arrays[which]
+        return pltpu.make_async_remote_copy(
+            src_ref=here.at[peer] if which == 0 else here,
+            dst_ref=there.at[slot],
+            send_sem=peer_send.at[which, k],
+            recv_sem=peer_recv.at[which, slot],
+            device_id={"dp": peer},
+            device_id_type=pl.DeviceIdType.MESH,
+        )
+
+    def push(k, _):
+        for which in (2, 1, 0):
+            peer_copy(which, k, lax.rem(me + k, n), me).start()
+        return 0
+
+    lax.fori_loop(1, n, push, 0)
+
+    def side_block(block):
+        return block + 2 - 4 * column
+
+    def from_side(block):
+        block_copy(side_block(block), 3, mate).wait_recv()
+        block_copy(side_block(block), 3, mate).start()
+
+    from_side(me)
+
+    def hop(step, _):
+        low, high = me - 4 * step, me + 4 * step
+
+        @pl.when(plane - step >= 0)
+        def _():
+            block_copy(low, 2, beside).wait_recv()
+
+            @pl.when(has_up)
+            def _():
+                block_copy(low, 0, me + 4).start()
+
+            block_copy(low, 2, beside).start()
+            block_copy(low, 3, mate).start()
+
+        @pl.when(plane + step < planes)
+        def _():
+            block_copy(high, 2, beside).wait_recv()
+
+            @pl.when(has_down)
+            def _():
+                block_copy(high, 1, me - 4).start()
+
+            block_copy(high, 2, beside).start()
+            block_copy(high, 3, mate).start()
+
+        @pl.when(plane - step >= 0)
+        def _():
+            from_side(low)
+
+        @pl.when(plane + step < planes)
+        def _():
+            from_side(high)
+
+        return 0
+
+    lax.fori_loop(1, planes, hop, 0)
+
+    def finish(at, _):
+        line = at * 4 + spot
+        block_copy(line, 2, beside).wait_send()
+        block_copy(line, 3, mate).wait_send()
+        block_copy(side_block(line), 3, mate).wait_send()
+        other = at * 4 + 1 - core
+        block_copy(other, 3, mate).wait_recv()
+        block_copy(other + 2, 3, mate).wait_recv()
+
+        @pl.when(has_up & (at <= plane))
+        def _():
+            block_copy(line, 0, me + 4).wait_send()
+
+        @pl.when(has_down & (at >= plane))
+        def _():
+            block_copy(line, 1, me - 4).wait_send()
+
+        return 0
+
+    lax.fori_loop(0, planes, finish, 0)
+
+    def settle(k, _):
+        for which in range(3):
+            peer_copy(which, k, lax.rem(me + k, n), me).wait_send()
+            peer_copy(which, k, lax.rem(me + k, n), lax.rem(me + n - k, n)).wait_recv()
+        return 0
+
+    lax.fori_loop(1, n, settle, 0)
+    for copy in owns:
+        copy.wait()
+
+
+def exchange(n, weight, rows, docs, info):
+    anywhere = pl.BlockSpec(memory_space=pl.ANY)
+    shape = jax.ShapeDtypeStruct
+    return pl.pallas_call(
+        functools.partial(exchange_kernel, n),
+        out_shape=(
+            shape((n * weight.shape[0], weight.shape[1]), weight.dtype),
+            shape(rows.shape, rows.dtype),
+            shape((n,) + docs.shape, docs.dtype),
+            shape((n,) + info.shape, info.dtype),
+        ),
+        in_specs=[anywhere] * 4,
+        out_specs=(anywhere,) * 4,
+        scratch_shapes=[
+            pltpu.SemaphoreType.DMA((4, n)),
+            pltpu.SemaphoreType.DMA((n,)),
+            pltpu.SemaphoreType.DMA((3, n)),
+            pltpu.SemaphoreType.DMA((3, n)),
+            pltpu.SemaphoreType.DMA((4,)),
+        ],
+        compiler_params=pltpu.CompilerParams(collective_id=0, has_side_effects=True),
+    )(weight, rows, docs, info)
+
+
 def shards(
     query_states, key_states, value_states, out_weight, token_ids, keep_flags, list_ids, owner_map
 ):
@@ -76,17 +254,13 @@
     me = lax.axis_index("dp").astype(jnp.int32)
     docs, length, features = query_states.shape
     rows = docs * length
-    cap = 3 * rows // (2 * n)
-    weight = lax.all_gather(out_weight, "dp", axis=0, tiled=True)
+    cap = -(-3 * rows // (2 * n) // 16) * 16
 
     lists = owner_map.shape[0]
     hit = list_ids.reshape(-1)[:, None] == jnp.arange(lists, dtype=jnp.int32)[None, :]
     owners = jnp.sum(jnp.where(hit, owner_map[None, :], 0), axis=1).reshape(docs, length)
     codes = jnp.where((keep_flags == 1)[:, None] & (token_ids != 0), owners, -1)
     info = jnp.concatenate([codes, jnp.broadcast_to(keep_flags[:, None], (docs, length))], axis=0)
-    every = lax.all_gather(info, "dp")
-    rank, mine, position, slot, keys = routing(every[:, :docs], every[:, docs:, 0], me)
-
     flat = codes.reshape(-1)
     member = (flat[None, :] == jnp.arange(n, dtype=jnp.int32)[:, None])
     at = jnp.arange(rows, dtype=jnp.int32)
@@ -99,15 +273,13 @@
 
     attended, pooled = attend(query_states, key_states, value_states, token_ids)
     packed = jnp.dot(pick, attended.reshape(rows, features), preferred_element_type=F32).astype(BF16)
-    arrived = lax.all_to_all(
-        packed.reshape(n, cap, features), "dp", split_axis=0, concat_axis=0, tiled=True
-    ).reshape(n * cap, features)
-    high = pooled.astype(BF16)
-    low = (pooled - high.astype(F32)).astype(BF16)
-    every_doc = lax.all_gather(jnp.concatenate([high, low], axis=0), "dp")
-    every_doc = jnp.concatenate([every_doc[:, :docs], every_doc[:, docs:]], axis=2).reshape(
-        n * docs, 2 * features
+    sent_docs = pooled.astype(BF16).reshape(16, docs * features // 16)
+    weight, arrived, every_doc, every = exchange(
+        n, out_weight, packed.reshape(n, cap, features), sent_docs, info
     )
+    arrived = arrived.reshape(n * cap, features)
+    every_doc = every_doc.reshape(n * docs, features)
+    rank, mine, position, slot, keys = routing(every[:, :docs], every[:, docs:, 0], me)
 
     mine_s = mine.reshape(n, rows)
     slot_s = jnp.where(mine_s, slot.reshape(n, rows), -1)
@@ -125,9 +297,7 @@
     wanted = jnp.arange(kept_slots, dtype=jnp.int32) * n + me
     picker = (rank[None, :] == wanted[:, None]).astype(BF16)
     chosen = jnp.dot(picker, every_doc, preferred_element_type=F32).astype(BF16)
-    parts = jnp.concatenate([chosen[:, :features], chosen[:, features:]], axis=0)
-    doc_sum = jnp.dot(parts, weight, preferred_element_type=F32)
-    doc_vectors = normalize(doc_sum[:kept_slots] + doc_sum[kept_slots:])
+    doc_vectors = normalize(jnp.dot(chosen, weight, preferred_element_type=F32))
     return (doc_vectors, token_vectors, token_keys)
 
 

time: 208 us -> 188 us (0.904)
  blocking collectives: 135 us -> 0 us
  Pallas kernels: 0 us -> 134 us
  between operations: 14.4 us -> 0.86 us
  starting transfers between devices: 7.48 us -> 0 us
  other arithmetic: 9.94 us -> 15.3 us
  matrix products: 24.7 us -> 22.4 us
    all_gather x2 -> x0, blocking collectives: 135 us -> none  [the longest x1 101 us: shards(): every = lax.all_gather(info, 'dp')]
    pallas_call x0 -> x1, Pallas kernels: none -> 134 us  [exchange(): pl.pallas_call(functools.partial(exchange_kernel, n), out_shape=(shape((n...]
    all_to_all x1 -> x0, starting transfers between devices: 7.45 us -> none  [shards(): lax.all_to_all(packed.reshape(n, cap, features), 'dp', split_axis=0, conc...]
    dot_general x2 -> x1, matrix products: 4.81 us -> 4.99 us  [shards(): doc_vectors = normalize(jnp.dot(chosen, weight, preferred_element_type=F32))]
  transfers between devices with their start and end apart: 2 -> 0, of which waited for: 0 -> 0; matrix products, arithmetic and copies ran while one was open for 16% -> 0% of each run, Pallas kernels for 0% -> 0%
where the time goes in v2:
time: 188 us
  Pallas kernels  134 us (71%)
  matrix products  22.4 us (12%)
  local copies, waits for them, and re-layouts  15.5 us (8%)
  other arithmetic  15.3 us (8%)
    pallas_call x1, Pallas kernels, exchange(): pl.pallas_call(functools.partial(exchange_kernel, n), out_shape=(shape((n...  134 us
    dot_general x1, matrix products, shards(): jnp.dot(sorted_rows, weight, preferred_element_type=F32)  11.5 us
    convert_element_type x2, local copies, waits for them, and re-layouts, attend(): attended = attended.reshape(doc_count, length, features).astype(BF16)  6.18 us
    dot_general x1, matrix products, shards(): doc_vectors = normalize(jnp.dot(chosen, weight, preferred_element_type=F32))  4.99 us
    convert_element_type x2, other arithmetic, normalize(): (values * lax.rsqrt(jnp.mean(values * values, axis=-1, keepdims=True) + 1...  4.49 us

profile of v2, /device:TPU:0, one launch (start us, length us, event | category | flops | bytes accessed | tf_op | source)
XLA Modules:
  0.0 187.6 jit_solution(1820383504357562263)
XLA Ops:
  0.6 0.7 broadcast_compare_fusion.1
  1.3 0.7 pad.1.clone
  3.1 0.8 convert_reduce_fusion.2
  3.9 1.1 select_reduce_fusion
  5.2 0.7 pad_add_fusion.info_ref
  6.5 1.2 reshape.263
  7.6 1.3 copy.43
  9.0 3.2 %reshape.264 = bf16[4,128,4,4,128]{4,3,2,1,0:T(4,128)(2,1)S(1)} reshape(bf16[4,128,2048]{2,1,0:T(8,128)(2,1)} %param.8) | data formatting | bytes 4194304 | tf_op jit(solution)/shard_map/reshape | solution.py:25
  12.2 0.7 fusion.5
  12.9 1.7 fusion.31
  14.6 0.7 fusion.11
  15.3 0.6 fusion.20
  16.7 2.9 %copy.30 = bf16[4,128,4,4,128]{4,3,2,1,0:T(4,128)(2,1)} copy(bf16[4,128,4,4,128]{1,4,3,2,0:T(8,128)(2,1)S(1)} %bitcast.58) | data formatting | bytes 4194304 | tf_op jit(solution)/shard_map/convert_element_type | solution.py:37
  19.6 3.3 %convert_element_type.63 = bf16[512,2048]{1,0:T(8,128)(2,1)S(1)} reshape(bf16[4,128,4,4,128]{4,3,2,1,0:T(4,128)(2,1)} %copy.30) | data formatting | bytes 4194304 | tf_op jit(solution)/shard_map/convert_element_type | solution.py:37
  22.9 3.5 %convolution_convert_fusion = bf16[768,2048]{1,0:T(8,128)(2,1)} fusion(pred[768,512]{1,0:T(8,128)(4,1)S(1)} %bitcast.62, bf16[512,2048]{1,0:T(8,128)(2,1)S(1)} %convert_element_type.63), kind=kOutput, calls=%fused_computation.9 | convolution fusion | flops 1612185600 | bytes 5636096 | tf_op jit(solution)/shard_map/dot_general | solution.py:275
  26.4 133.5 %shard_map.103 = (bf16[2048,2048]{1,0:T(8,128)(2,1)}, bf16[16,48,2048]{2,1,0:T(8,128)(2,1)}, bf16[16,16,512]{2,1,0:T(8,128)(2,1)}, s32[16,8,128]{2,1,0:T(8,128)}) custom-call(bf16[128,2048]{1,0:T(8,128)(2,1)} %w_ref.1, bf16[16,48,2048]{2,1,0:T(8,128)(2,1)} %bitcast.59, bf16[16,512]{1,0:T(8,128)(2,1)} %reshape.267.docs_ref, s32[8,128]{1,0:T(8,128)} %pad_add_fusion.info_ref), custom_call_target="tpu_custom_call" | custom-call | tf_op jit(solution)/shard_map/pallas_call | solution.py:229
  159.9 1.1 reshape.268
  161.0 1.2 fusion.30
  162.2 1.2 convert_reduce_fusion
  164.1 5.0 %multiply_reduce_fusion.1 = (f32[3]{0:T(128)S(1)}, f32[3,2048]{1,0:T(4,128)S(1)}) fusion(bf16[2048,2048]{1,0:T(8,128)(2,1)} %get-tuple-element.9, bf16[64,2048]{1,0:T(8,128)(2,1)S(1)} %reshape.268, s32[64]{0:T(128)S(1)} %broadcast_select_fusion, s32[3]{0:T(128)S(1)} %copy-done), kind=kOutput, calls=%fused_computation.44 | convolution fusion | flops 25970876 | bytes 8675608 | tf_op jit(solution)/shard_map/dot_general | solution.py:300
  169.1 0.7 multiply_convert_fusion.1
  170.6 0.7 select_reduce_fusion.2
  171.4 11.5 %multiply_reduce_fusion = (f32[512]{0:T(512)S(1)}, f32[512,2048]{1,0:T(8,128)}) fusion(bf16[2048,2048]{1,0:T(8,128)(2,1)} %get-tuple-element.9, bf16[768,2048]{1,0:T(8,128)(2,1)S(1)} %bitcast.68, s32[768]{0:T(1024)S(1)} %sub.21), kind=kOutput, calls=%fused_computation.6 | convolution fusion | flops 5909118464 | bytes 15733760 | tf_op jit(solution)/shard_map/dot_general | solution.py:294
  183.8 3.8 %multiply_convert_fusion = bf16[512,2048]{1,0:T(8,128)(2,1)} fusion(f32[512,2048]{1,0:T(8,128)} %get-tuple-element.28, f32[512]{0:T(512)S(1)} %add_rsqrt_fusion), kind=kLoop, calls=%fused_computation.5 | loop fusion | flops 2097152 | bytes 6293504 | tf_op jit(solution)/shard_map/convert_element_type | solution.py:17
  (44 shorter events, 4.9 us)
Async XLA Ops:
  26.4 137.4 %copy-start.1 = (pred[4,4]{1,0:T(4,128)(4,1)S(1)}, pred[4,4]{1,0:T(4,128)(4,1)}, u32[]{:S(2)}) copy-start(pred[4,4]{1,0:T(4,128)(4,1)} %iota_compare_fusion.12) | copy-start | bytes 52
  26.4 137.7 %copy-start = (s32[3]{0:T(128)S(1)}, s32[3]{0:T(128)}, u32[]{:S(2)}) copy-start(s32[3]{0:T(128)} %multiply_add_fusion) | copy-start | bytes 40
  164.1 7.3 %copy-start.2 = (bf16[16,48,2048]{2,1,0:T(8,128)(2,1)S(1)}, bf16[16,48,2048]{2,1,0:T(8,128)(2,1)}, u32[]{:S(2)}) copy-start(bf16[16,48,2048]{2,1,0:T(8,128)(2,1)} %get-tuple-element.10) | copy-start | bytes 9437188

commit v3 on v2

--- a/solution.py
+++ b/solution.py
@@ -138,12 +138,25 @@
             device_id_type=pl.DeviceIdType.MESH,
         )
 
-    def push(k, _):
-        for which in (2, 1, 0):
-            peer_copy(which, k, lax.rem(me + k, n), me).start()
-        return 0
-
-    lax.fori_loop(1, n, push, 0)
+    def target(k):
+        ahead = lax.rem(plane + lax.div(k, 4), planes)
+        return ahead * 4 + lax.rem(spot + lax.rem(k, 4), 4)
+
+    def origin(k):
+        behind = lax.rem(plane + planes - lax.div(k, 4), planes)
+        return behind * 4 + lax.rem(spot + 4 - lax.rem(k, 4), 4)
+
+    def push_small(k, _):
+        for which in (2, 1):
+            peer_copy(which, k, target(k), me).start()
+        return 0
+
+    def push_rows(k, _):
+        peer_copy(0, k, target(k), me).start()
+        return 0
+
+    lax.fori_loop(1, n, push_small, 0)
+    lax.fori_loop(1, 4, push_rows, 0)
 
     def side_block(block):
         return block + 2 - 4 * column
@@ -178,6 +191,8 @@
 
             block_copy(high, 2, beside).start()
             block_copy(high, 3, mate).start()
+
+        lax.fori_loop(4 * step, 4 * step + 4, push_rows, 0)
 
         @pl.when(plane - step >= 0)
         def _():
@@ -214,8 +229,8 @@
 
     def settle(k, _):
         for which in range(3):
-            peer_copy(which, k, lax.rem(me + k, n), me).wait_send()
-            peer_copy(which, k, lax.rem(me + k, n), lax.rem(me + n - k, n)).wait_recv()
+            peer_copy(which, k, target(k), me).wait_send()
+            peer_copy(which, k, target(k), origin(k)).wait_recv()
         return 0
 
     lax.fori_loop(1, n, settle, 0)

time: 188 us -> 179 us (0.952)
  Pallas kernels: 134 us -> 125 us
    pallas_call x1, Pallas kernels: 134 us -> 125 us  [exchange(): pl.pallas_call(functools.partial(exchange_kernel, n), out_shape=(shape((n...]
where the time goes in v3:
time: 179 us
  Pallas kernels  125 us (70%)
  matrix products  22.4 us (13%)
  local copies, waits for them, and re-layouts  15.5 us (9%)
  other arithmetic  15.3 us (9%)
    pallas_call x1, Pallas kernels, exchange(): pl.pallas_call(functools.partial(exchange_kernel, n), out_shape=(shape((n...  125 us
    dot_general x1, matrix products, shards(): jnp.dot(sorted_rows, weight, preferred_element_type=F32)  11.5 us
    convert_element_type x2, local copies, waits for them, and re-layouts, attend(): attended = attended.reshape(doc_count, length, features).astype(BF16)  6.18 us
    dot_general x1, matrix products, shards(): doc_vectors = normalize(jnp.dot(chosen, weight, preferred_element_type=F32))  4.99 us
    convert_element_type x2, other arithmetic, normalize(): (values * lax.rsqrt(jnp.mean(values * values, axis=-1, keepdims=True) + 1...  4.49 us

profile of v3, /device:TPU:0, one launch (start us, length us, event | category | flops | bytes accessed | tf_op | source)
XLA Modules:
  0.0 178.7 jit_solution(6435259857301021555)
XLA Ops:
  0.6 0.7 broadcast_compare_fusion.1
  1.3 0.7 pad.1.clone
  3.1 0.8 convert_reduce_fusion.2
  3.9 1.1 select_reduce_fusion
  5.2 0.7 pad_add_fusion.info_ref
  6.5 1.2 reshape.263
  7.6 1.3 copy.43
  9.0 3.2 %reshape.264 = bf16[4,128,4,4,128]{4,3,2,1,0:T(4,128)(2,1)S(1)} reshape(bf16[4,128,2048]{2,1,0:T(8,128)(2,1)} %param.8) | data formatting | bytes 4194304 | tf_op jit(solution)/shard_map/reshape | solution.py:25
  12.2 0.7 fusion.5
  12.9 1.7 fusion.31
  14.6 0.7 fusion.11
  15.3 0.6 fusion.20
  16.7 2.9 %copy.30 = bf16[4,128,4,4,128]{4,3,2,1,0:T(4,128)(2,1)} copy(bf16[4,128,4,4,128]{1,4,3,2,0:T(8,128)(2,1)S(1)} %bitcast.58) | data formatting | bytes 4194304 | tf_op jit(solution)/shard_map/convert_element_type | solution.py:37
  19.6 3.3 %convert_element_type.63 = bf16[512,2048]{1,0:T(8,128)(2,1)S(1)} reshape(bf16[4,128,4,4,128]{4,3,2,1,0:T(4,128)(2,1)} %copy.30) | data formatting | bytes 4194304 | tf_op jit(solution)/shard_map/convert_element_type | solution.py:37
  22.9 3.5 %convolution_convert_fusion = bf16[768,2048]{1,0:T(8,128)(2,1)} fusion(pred[768,512]{1,0:T(8,128)(4,1)S(1)} %bitcast.62, bf16[512,2048]{1,0:T(8,128)(2,1)S(1)} %convert_element_type.63), kind=kOutput, calls=%fused_computation.9 | convolution fusion | flops 1612185600 | bytes 5636096 | tf_op jit(solution)/shard_map/dot_general | solution.py:290
  26.4 124.7 %shard_map.103 = (bf16[2048,2048]{1,0:T(8,128)(2,1)}, bf16[16,48,2048]{2,1,0:T(8,128)(2,1)}, bf16[16,16,512]{2,1,0:T(8,128)(2,1)}, s32[16,8,128]{2,1,0:T(8,128)}) custom-call(bf16[128,2048]{1,0:T(8,128)(2,1)} %w_ref.1, bf16[16,48,2048]{2,1,0:T(8,128)(2,1)} %bitcast.59, bf16[16,512]{1,0:T(8,128)(2,1)} %reshape.267.docs_ref, s32[8,128]{1,0:T(8,128)} %pad_add_fusion.info_ref), custom_call_target="tpu_custom_call" | custom-call | tf_op jit(solution)/shard_map/pallas_call | solution.py:244
  151.1 1.1 reshape.268
  152.2 1.2 fusion.30
  153.4 1.2 convert_reduce_fusion
  155.3 5.0 %multiply_reduce_fusion.1 = (f32[3]{0:T(128)S(1)}, f32[3,2048]{1,0:T(4,128)S(1)}) fusion(bf16[2048,2048]{1,0:T(8,128)(2,1)} %get-tuple-element.9, bf16[64,2048]{1,0:T(8,128)(2,1)S(1)} %reshape.268, s32[64]{0:T(128)S(1)} %broadcast_select_fusion, s32[3]{0:T(128)S(1)} %copy-done), kind=kOutput, calls=%fused_computation.44 | convolution fusion | flops 25970876 | bytes 8675608 | tf_op jit(solution)/shard_map/dot_general | solution.py:315
  160.3 0.7 multiply_convert_fusion.1
  161.7 0.7 select_reduce_fusion.2
  162.6 11.5 %multiply_reduce_fusion = (f32[512]{0:T(512)S(1)}, f32[512,2048]{1,0:T(8,128)}) fusion(bf16[2048,2048]{1,0:T(8,128)(2,1)} %get-tuple-element.9, bf16[768,2048]{1,0:T(8,128)(2,1)S(1)} %bitcast.68, s32[768]{0:T(1024)S(1)} %sub.21), kind=kOutput, calls=%fused_computation.6 | convolution fusion | flops 5909118464 | bytes 15733760 | tf_op jit(solution)/shard_map/dot_general | solution.py:309
  175.0 3.8 %multiply_convert_fusion = bf16[512,2048]{1,0:T(8,128)(2,1)} fusion(f32[512,2048]{1,0:T(8,128)} %get-tuple-element.28, f32[512]{0:T(512)S(1)} %add_rsqrt_fusion), kind=kLoop, calls=%fused_computation.5 | loop fusion | flops 2097152 | bytes 6293504 | tf_op jit(solution)/shard_map/convert_element_type | solution.py:17
  (44 shorter events, 4.9 us)
Async XLA Ops:
  26.4 128.6 %copy-start.1 = (pred[4,4]{1,0:T(4,128)(4,1)S(1)}, pred[4,4]{1,0:T(4,128)(4,1)}, u32[]{:S(2)}) copy-start(pred[4,4]{1,0:T(4,128)(4,1)} %iota_compare_fusion.12) | copy-start | bytes 52
  26.4 128.9 %copy-start = (s32[3]{0:T(128)S(1)}, s32[3]{0:T(128)}, u32[]{:S(2)}) copy-start(s32[3]{0:T(128)} %multiply_add_fusion) | copy-start | bytes 40
  155.3 7.3 %copy-start.2 = (bf16[16,48,2048]{2,1,0:T(8,128)(2,1)S(1)}, bf16[16,48,2048]{2,1,0:T(8,128)(2,1)}, u32[]{:S(2)}) copy-start(bf16[16,48,2048]{2,1,0:T(8,128)(2,1)} %get-tuple-element.10) | copy-start | bytes 9437188

commit v4 on v3

--- a/solution.py
+++ b/solution.py
@@ -262,6 +262,28 @@
     )(weight, rows, docs, info)
 
 
+def place_kernel(position_ref, arrived_ref, w_ref, out_ref):
+    tile = out_ref.shape[0]
+    row = lax.broadcasted_iota(jnp.int32, (tile, position_ref.shape[1]), 0) + pl.program_id(0) * tile
+    order = jnp.where(row == position_ref[...], 1.0, 0.0).astype(BF16)
+    chosen = jnp.dot(order, arrived_ref[...], preferred_element_type=F32).astype(BF16)
+    out_ref[...] = normalize(jnp.dot(chosen, w_ref[...], preferred_element_type=F32))
+
+
+def place(rows, positions, arrived, weight):
+    width = weight.shape[1]
+    tile = min(rows, 256)
+    whole = lambda array: pl.BlockSpec(array.shape, lambda i: (0, 0))
+    return pl.pallas_call(
+        place_kernel,
+        grid=(rows // tile,),
+        out_shape=jax.ShapeDtypeStruct((rows, width), BF16),
+        in_specs=[whole(positions), whole(arrived), whole(weight)],
+        out_specs=pl.BlockSpec((tile, width), lambda i: (i, 0)),
+        compiler_params=pltpu.CompilerParams(vmem_limit_bytes=50 * 2**20),
+    )(positions, arrived, weight)
+
+
 def shards(
     query_states, key_states, value_states, out_weight, token_ids, keep_flags, list_ids, owner_map
 ):
@@ -305,8 +327,7 @@
     slot_key = jnp.sum(jnp.where(fits, keys.reshape(n, 1, rows) + 1, 0), axis=2).reshape(-1)
     order = jnp.arange(rows, dtype=jnp.int32)[:, None] == slot_position[None, :]
     token_keys = jnp.sum(jnp.where(order, slot_key[None, :], 0), axis=1) - 1
-    sorted_rows = jnp.dot(order.astype(BF16), arrived, preferred_element_type=F32).astype(BF16)
-    token_vectors = normalize(jnp.dot(sorted_rows, weight, preferred_element_type=F32))
+    token_vectors = place(rows, slot_position[None, :], arrived, weight)
 
     kept_slots = 3 * docs // 4
     wanted = jnp.arange(kept_slots, dtype=jnp.int32) * n + me

time: 179 us -> 178 us (level)
  Pallas kernels: 125 us -> 135 us
  matrix products: 22.4 us -> 14.5 us
  other arithmetic: 15.3 us -> 11.6 us
    dot_general x1 -> x0, matrix products: 11.5 us -> none  [shards(): jnp.dot(sorted_rows, weight, preferred_element_type=F32)]
    pallas_call x0 -> x1, Pallas kernels: none -> 11 us  [place(): pl.pallas_call(place_kernel, grid=(rows // tile,), out_shape=jax.ShapeDty...]
    convert_element_type x2 -> x1, other arithmetic: 4.49 us -> 0.69 us  [normalize(): (values * lax.rsqrt(jnp.mean(values * values, axis=-1, keepdims=True) + 1...]
    dot_general x1, matrix products: 0.7 us -> 2.89 us  [attend(): jnp.einsum('nhgqs,nshd->nqhgd', weights, values_split, preferred_element_...]
    unnamed x6 -> x10, local copies, waits for them, and re-layouts: 0.01 us -> 1.9 us
where the time goes in v4:
time: 178 us; the launch traced here: 177 us
  Pallas kernels  135 us (76%)
  local copies, waits for them, and re-layouts  15.1 us (8%)
  matrix products  14.5 us (8%)
  other arithmetic  11.6 us (7%)
    pallas_call x1, Pallas kernels, exchange(): pl.pallas_call(functools.partial(exchange_kernel, n), out_shape=(shape((n...  124 us
    pallas_call x1, Pallas kernels, place(): pl.pallas_call(place_kernel, grid=(rows // tile,), out_shape=jax.ShapeDty...  11 us
    convert_element_type x2, local copies, waits for them, and re-layouts, attend(): attended = attended.reshape(doc_count, length, features).astype(BF16)  7.37 us
    dot_general x1, matrix products, shards(): jnp.dot(pick, attended.reshape(rows, features), preferred_element_type=F32)  5.14 us
    dot_general x1, matrix products, shards(): doc_vectors = normalize(jnp.dot(chosen, weight, preferred_element_type=F32))  4.84 us

profile of v4, /device:TPU:0, one launch (start us, length us, event | category | flops | bytes accessed | tf_op | source)
XLA Modules:
  0.0 177.5 jit_solution(8690518385023850213)
XLA Ops:
  0.6 0.8 convert_reduce_fusion.2
  1.4 1.1 select_reduce_fusion
  2.6 0.7 broadcast_compare_fusion.1
  3.5 0.3 fusion.12
  3.8 3.3 %reshape.264 = bf16[4,128,4,4,128]{4,3,2,1,0:T(4,128)(2,1)S(1)} reshape(bf16[4,128,2048]{2,1,0:T(8,128)(2,1)} %param.8) | data formatting | bytes 4194304 | tf_op jit(solution)/shard_map/reshape | solution.py:25
  7.2 0.7 fusion.5
  8.0 2.9 %fusion.28 = (f32[4,4,4,128]{3,2,1,0:T(4,128)S(1)}, f32[4,4,4,128,128]{3,4,2,1,0:T(8,128)}) fusion(f32[4,4,128,128,4]{3,2,4,1,0:T(8,128)S(1)} %fusion.5, pred[4,128]{1,0:T(4,128)(4,1)S(1)} %get-tuple-element.20), kind=kOutput, calls=%fused_computation.71 | output fusion | flops 6291583 | bytes 8421888 | tf_op jit(solution)/shard_map/sub | solution.py:34
  10.9 0.3 copy.43
  11.2 2.9 %fusion.11 = bf16[4,4,4,128,128]{3,4,2,1,0:T(8,128)(2,1)S(1)} fusion(bf16[4,128,4,128,1]{1,3,4,2,0:T(8,128)(2,1)S(1)} %bitcast.60, f32[4,4,4,128,128]{3,4,2,1,0:T(8,128)} %get-tuple-element.24, f32[4,4,4,128]{3,2,1,0:T(4,128)S(1)} %get-tuple-element.23), kind=kOutput, calls=%fused_computation.17 | convolution fusion | flops 271581184 | bytes 6848512 | tf_op jit(solution)/shard_map/nhgqs,nshd->nqhgd/dot_general | solution.py:36
  14.1 2.9 %copy.30 = bf16[4,128,4,4,128]{4,3,2,1,0:T(4,128)(2,1)} copy(bf16[4,128,4,4,128]{1,4,3,2,0:T(8,128)(2,1)S(1)} %bitcast.56) | data formatting | bytes 4194304 | tf_op jit(solution)/shard_map/convert_element_type | solution.py:37
  17.0 4.5 %convert_element_type.56 = bf16[512,2048]{1,0:T(8,128)(2,1)} reshape(bf16[4,128,4,4,128]{4,3,2,1,0:T(4,128)(2,1)} %copy.30) | data formatting | bytes 4194304 | tf_op jit(solution)/shard_map/convert_element_type | solution.py:37
  21.4 5.1 %convolution_convert_fusion = bf16[768,2048]{1,0:T(8,128)(2,1)} fusion(pred[768,512]{1,0:T(8,128)(4,1)S(1)} %bitcast.61, bf16[512,2048]{1,0:T(8,128)(2,1)} %convert_element_type.56), kind=kOutput, calls=%fused_computation.7 | convolution fusion | flops 1612185600 | bytes 5636096 | tf_op jit(solution)/shard_map/dot_general | solution.py:312
  26.6 0.6 fusion.17
  27.3 0.6 reshape.267.docs_ref
  28.1 0.7 pad_add_fusion.info_ref
  28.8 124.4 %shard_map.103 = (bf16[2048,2048]{1,0:T(8,128)(2,1)}, bf16[16,48,2048]{2,1,0:T(8,128)(2,1)}, bf16[16,16,512]{2,1,0:T(8,128)(2,1)}, s32[16,8,128]{2,1,0:T(8,128)}) custom-call(bf16[128,2048]{1,0:T(8,128)(2,1)} %w_ref.1, bf16[16,48,2048]{2,1,0:T(8,128)(2,1)} %bitcast.58, bf16[16,512]{1,0:T(8,128)(2,1)} %reshape.267.docs_ref, s32[8,128]{1,0:T(8,128)} %pad_add_fusion.info_ref), custom_call_target="tpu_custom_call" | custom-call | tf_op jit(solution)/shard_map/pallas_call | solution.py:244
  153.2 1.2 convert_reduce_fusion
  154.4 1.2 fusion.27
  157.1 0.7 select_reduce_fusion.2
  158.2 0.6 broadcast_add_fusion.2
  158.9 1.9 %copy-done = bf16[16,48,2048]{2,1,0:T(8,128)(2,1)S(1)} copy-done((bf16[16,48,2048]{2,1,0:T(8,128)(2,1)S(1)}, bf16[16,48,2048]{2,1,0:T(8,128)(2,1)}, u32[]{:S(2)}) %copy-start) | copy-done | bytes 3145752
  160.7 11.0 %shard_map.104 = bf16[512,2048]{1,0:T(8,128)(2,1)} custom-call(s32[1,768]{1,0:T(1,128)S(1)} %sub.23.position_ref, bf16[768,2048]{1,0:T(8,128)(2,1)S(1)} %bitcast.55, bf16[2048,2048]{1,0:T(8,128)(2,1)} %get-tuple-element.9.w_ref), custom_call_target="tpu_custom_call" | custom-call | tf_op jit(solution)/shard_map/pallas_call | solution.py:277
  171.9 4.8 %multiply_reduce_fusion = (f32[3]{0:T(128)S(1)}, f32[3,2048]{1,0:T(4,128)S(1)}) fusion(bf16[2048,2048]{1,0:T(8,128)(2,1)} %get-tuple-element.9.w_ref, bf16[64,2048]{1,0:T(8,128)(2,1)S(1)} %reshape.268, s32[64]{0:T(128)S(1)} %broadcast_select_fusion, s32[3]{0:T(128)S(1)} %multiply_add_fusion), kind=kOutput, calls=%fused_computation.39 | convolution fusion | flops 25970876 | bytes 8675608 | tf_op jit(solution)/shard_map/dot_general | solution.py:336
  176.8 0.7 multiply_convert_fusion
  (47 shorter events, 2.7 us)
Async XLA Ops:
  3.8 3.3 %copy-start.1 = (bf16[4,128,512]{2,1,0:T(8,128)(2,1)S(1)}, bf16[4,128,512]{2,1,0:T(8,128)(2,1)}, u32[]{:S(2)}) copy-start(bf16[4,128,512]{2,1,0:T(8,128)(2,1)} %param.9) | copy-start | bytes 1572868
  8.0 2.9 %copy-start.2 = (bf16[4,128,512]{2,1,0:T(8,128)(2,1)S(1)}, bf16[4,128,512]{2,1,0:T(8,128)(2,1)}, u32[]{:S(2)}) copy-start(bf16[4,128,512]{2,1,0:T(8,128)(2,1)} %param.10) | copy-start | bytes 1572868
  26.6 1.4 copy-start.4
  158.8 1.9 %copy-start = (bf16[16,48,2048]{2,1,0:T(8,128)(2,1)S(1)}, bf16[16,48,2048]{2,1,0:T(8,128)(2,1)}, u32[]{:S(2)}) copy-start(bf16[16,48,2048]{2,1,0:T(8,128)(2,1)} %get-tuple-element.10) | copy-start | bytes 9437188
  160.7 11.0 %copy-start.3 = (bf16[16,16,512]{2,1,0:T(8,128)(2,1)S(1)}, bf16[16,16,512]{2,1,0:T(8,128)(2,1)}, u32[]{:S(2)}) copy-start(bf16[16,16,512]{2,1,0:T(8,128)(2,1)} %get-tuple-element.8) | copy-start | bytes 786436

commit v5 on v4

--- a/solution.py
+++ b/solution.py
@@ -262,26 +262,35 @@
     )(weight, rows, docs, info)
 
 
-def place_kernel(position_ref, arrived_ref, w_ref, out_ref):
+def place_kernel(position_ref, arrived_ref, docs_ref, w_ref, out_ref, docs_out_ref):
     tile = out_ref.shape[0]
     row = lax.broadcasted_iota(jnp.int32, (tile, position_ref.shape[1]), 0) + pl.program_id(0) * tile
     order = jnp.where(row == position_ref[...], 1.0, 0.0).astype(BF16)
     chosen = jnp.dot(order, arrived_ref[...], preferred_element_type=F32).astype(BF16)
-    out_ref[...] = normalize(jnp.dot(chosen, w_ref[...], preferred_element_type=F32))
-
-
-def place(rows, positions, arrived, weight):
+    both = jnp.concatenate([chosen, docs_ref[...]], axis=0)
+    unit = normalize(jnp.dot(both, w_ref[...], preferred_element_type=F32))
+    out_ref[...] = unit[:tile]
+    docs_out_ref[...] = unit[tile:]
+
+
+def place(rows, positions, arrived, doc_rows, weight):
     width = weight.shape[1]
     tile = min(rows, 256)
     whole = lambda array: pl.BlockSpec(array.shape, lambda i: (0, 0))
     return pl.pallas_call(
         place_kernel,
         grid=(rows // tile,),
-        out_shape=jax.ShapeDtypeStruct((rows, width), BF16),
-        in_specs=[whole(positions), whole(arrived), whole(weight)],
-        out_specs=pl.BlockSpec((tile, width), lambda i: (i, 0)),
+        out_shape=(
+            jax.ShapeDtypeStruct((rows, width), BF16),
+            jax.ShapeDtypeStruct((doc_rows.shape[0], width), BF16),
+        ),
+        in_specs=[whole(positions), whole(arrived), whole(doc_rows), whole(weight)],
+        out_specs=(
+            pl.BlockSpec((tile, width), lambda i: (i, 0)),
+            pl.BlockSpec((doc_rows.shape[0], width), lambda i: (0, 0)),
+        ),
         compiler_params=pltpu.CompilerParams(vmem_limit_bytes=50 * 2**20),
-    )(positions, arrived, weight)
+    )(positions, arrived, doc_rows, weight)
 
 
 def shards(
@@ -327,13 +336,14 @@
     slot_key = jnp.sum(jnp.where(fits, keys.reshape(n, 1, rows) + 1, 0), axis=2).reshape(-1)
     order = jnp.arange(rows, dtype=jnp.int32)[:, None] == slot_position[None, :]
     token_keys = jnp.sum(jnp.where(order, slot_key[None, :], 0), axis=1) - 1
-    token_vectors = place(rows, slot_position[None, :], arrived, weight)
-
     kept_slots = 3 * docs // 4
-    wanted = jnp.arange(kept_slots, dtype=jnp.int32) * n + me
+    held = -(-kept_slots // 16) * 16
+    slots = jnp.arange(held, dtype=jnp.int32)
+    wanted = jnp.where(slots < kept_slots, slots * n + me, n * docs)
     picker = (rank[None, :] == wanted[:, None]).astype(BF16)
     chosen = jnp.dot(picker, every_doc, preferred_element_type=F32).astype(BF16)
-    doc_vectors = normalize(jnp.dot(chosen, weight, preferred_element_type=F32))
+    token_vectors, unit_docs = place(rows, slot_position[None, :], arrived, chosen, weight)
+    doc_vectors = unit_docs[:kept_slots]
     return (doc_vectors, token_vectors, token_keys)
 
 

time: 178 us -> 175 us (0.983)
  matrix products: 14.5 us -> 9.87 us
    dot_general x1, matrix products: 4.84 us -> 0.2 us  [shards(): chosen = jnp.dot(picker, every_doc, preferred_element_type=F32).astype(BF16)]
where the time goes in v5:
time: 175 us; the launch traced here: 174 us
  Pallas kernels  136 us (78%)
  local copies, waits for them, and re-layouts  16.6 us (9%)
  other arithmetic  10.9 us (6%)
  matrix products  9.87 us (6%)
    pallas_call x1, Pallas kernels, exchange(): pl.pallas_call(functools.partial(exchange_kernel, n), out_shape=(shape((n...  124 us
    pallas_call x1, Pallas kernels, place(): pl.pallas_call(place_kernel, grid=(rows // tile,), out_shape=(jax.ShapeDt...  11.2 us
    convert_element_type x2, local copies, waits for them, and re-layouts, attend(): attended = attended.reshape(doc_count, length, features).astype(BF16)  7.37 us
    dot_general x1, matrix products, shards(): jnp.dot(pick, attended.reshape(rows, features), preferred_element_type=F32)  5.14 us

profile of v5, /device:TPU:0, one launch (start us, length us, event | category | flops | bytes accessed | tf_op | source)
XLA Modules:
  0.0 173.9 jit_solution(11672168497640432510)
XLA Ops:
  0.6 0.8 convert_reduce_fusion.2
  1.4 1.1 select_reduce_fusion
  2.6 0.7 broadcast_compare_fusion.1
  3.5 0.3 fusion.12
  3.8 3.3 %reshape.259 = bf16[4,128,4,4,128]{4,3,2,1,0:T(4,128)(2,1)S(1)} reshape(bf16[4,128,2048]{2,1,0:T(8,128)(2,1)} %param.8) | data formatting | bytes 4194304 | tf_op jit(solution)/shard_map/reshape | solution.py:25
  7.2 0.7 fusion.5
  8.0 2.9 %fusion.24 = (f32[4,4,4,128]{3,2,1,0:T(4,128)S(1)}, f32[4,4,4,128,128]{3,4,2,1,0:T(8,128)}) fusion(f32[4,4,128,128,4]{3,2,4,1,0:T(8,128)S(1)} %fusion.5, pred[4,128]{1,0:T(4,128)(4,1)S(1)} %get-tuple-element.24), kind=kOutput, calls=%fused_computation.67 | output fusion | flops 6291583 | bytes 8421888 | tf_op jit(solution)/shard_map/sub | solution.py:34
  10.9 0.3 copy.43
  11.2 2.9 %fusion.11 = bf16[4,4,4,128,128]{3,4,2,1,0:T(8,128)(2,1)S(1)} fusion(bf16[4,128,4,128,1]{1,3,4,2,0:T(8,128)(2,1)S(1)} %bitcast.59, f32[4,4,4,128,128]{3,4,2,1,0:T(8,128)} %get-tuple-element.28, f32[4,4,4,128]{3,2,1,0:T(4,128)S(1)} %get-tuple-element.27), kind=kOutput, calls=%fused_computation.17 | convolution fusion | flops 271581184 | bytes 6848512 | tf_op jit(solution)/shard_map/nhgqs,nshd->nqhgd/dot_general | solution.py:36
  14.1 2.9 %copy.30 = bf16[4,128,4,4,128]{4,3,2,1,0:T(4,128)(2,1)} copy(bf16[4,128,4,4,128]{1,4,3,2,0:T(8,128)(2,1)S(1)} %bitcast.55) | data formatting | bytes 4194304 | tf_op jit(solution)/shard_map/convert_element_type | solution.py:37
  17.0 4.5 %convert_element_type.53 = bf16[512,2048]{1,0:T(8,128)(2,1)} reshape(bf16[4,128,4,4,128]{4,3,2,1,0:T(4,128)(2,1)} %copy.30) | data formatting | bytes 4194304 | tf_op jit(solution)/shard_map/convert_element_type | solution.py:37
  21.4 5.1 %convolution_convert_fusion = bf16[768,2048]{1,0:T(8,128)(2,1)} fusion(pred[768,512]{1,0:T(8,128)(4,1)S(1)} %bitcast.60, bf16[512,2048]{1,0:T(8,128)(2,1)} %convert_element_type.53), kind=kOutput, calls=%fused_computation.7 | convolution fusion | flops 1612185600 | bytes 5636096 | tf_op jit(solution)/shard_map/dot_general | solution.py:321
  26.6 0.6 fusion.16
  27.3 0.6 reshape.262.docs_ref
  28.1 0.7 pad_add_fusion.info_ref
  28.8 124.4 %shard_map.103 = (bf16[2048,2048]{1,0:T(8,128)(2,1)}, bf16[16,48,2048]{2,1,0:T(8,128)(2,1)}, bf16[16,16,512]{2,1,0:T(8,128)(2,1)}, s32[16,8,128]{2,1,0:T(8,128)}) custom-call(bf16[128,2048]{1,0:T(8,128)(2,1)} %w_ref.1, bf16[16,48,2048]{2,1,0:T(8,128)(2,1)} %bitcast.57, bf16[16,512]{1,0:T(8,128)(2,1)} %reshape.262.docs_ref, s32[8,128]{1,0:T(8,128)} %pad_add_fusion.info_ref), custom_call_target="tpu_custom_call" | custom-call | tf_op jit(solution)/shard_map/pallas_call | solution.py:244
  153.2 1.2 convert_reduce_fusion.1
  154.4 1.2 fusion.23
  157.1 0.7 select_reduce_fusion.2
  158.2 0.6 broadcast_add_fusion.2
  158.8 1.1 reshape.266
  160.2 1.9 %copy-done = bf16[16,48,2048]{2,1,0:T(8,128)(2,1)S(1)} copy-done((bf16[16,48,2048]{2,1,0:T(8,128)(2,1)S(1)}, bf16[16,48,2048]{2,1,0:T(8,128)(2,1)}, u32[]{:S(2)}) %copy-start) | copy-done | bytes 3145752
  162.1 11.2 %shard_map.104 = (bf16[512,2048]{1,0:T(8,128)(2,1)}, bf16[16,2048]{1,0:T(8,128)(2,1)S(1)}) custom-call(s32[1,768]{1,0:T(1,128)S(1)} %sub.23.position_ref, bf16[768,2048]{1,0:T(8,128)(2,1)S(1)} %bitcast.54, bf16[16,2048]{1,0:T(8,128)(2,1)S(1)} %convolution_convert_fusion.1.docs_ref, bf16[2048,2048]{1,0:T(8,128)(2,1)} %get-tuple-element.12.w_ref), custom_call_target="tpu_custom_call" | custom-call | tf_op jit(solution)/shard_map/pallas_call | solution.py:280
  173.3 0.6 slice.11
  (44 shorter events, 2.8 us)
Async XLA Ops:
  3.8 3.3 %copy-start.1 = (bf16[4,128,512]{2,1,0:T(8,128)(2,1)S(1)}, bf16[4,128,512]{2,1,0:T(8,128)(2,1)}, u32[]{:S(2)}) copy-start(bf16[4,128,512]{2,1,0:T(8,128)(2,1)} %param.9) | copy-start | bytes 1572868
  7.9 2.9 %copy-start.2 = (bf16[4,128,512]{2,1,0:T(8,128)(2,1)S(1)}, bf16[4,128,512]{2,1,0:T(8,128)(2,1)}, u32[]{:S(2)}) copy-start(bf16[4,128,512]{2,1,0:T(8,128)(2,1)} %param.10) | copy-start | bytes 1572868
  26.6 1.4 copy-start.3
  160.2 1.9 %copy-start = (bf16[16,48,2048]{2,1,0:T(8,128)(2,1)S(1)}, bf16[16,48,2048]{2,1,0:T(8,128)(2,1)}, u32[]{:S(2)}) copy-start(bf16[16,48,2048]{2,1,0:T(8,128)(2,1)} %get-tuple-element.10) | copy-start | bytes 9437188
